TPU v7x, 512 devices: a whole 4x4x16 slice. The times are simulated.
512 devices in a mesh: tm: 32 (over z, core), state: 16 (over y, x).
Axes of the slice: x: 4, y: 4, z: 16, core: 2. Of those that a mesh axis runs over, the one named last changes fastest.
Arguments:
- transition: float32 [1024, 1024], replicated, may hold values from -0.1 to 1.1
- prior_cov: float32 [1024, 1024], replicated, may hold values from -0.1 to 3.5, as said below
- noise_var: float32 [1024], replicated, may hold values from 0.2 to 30
- sensor_mask: int32 [32, 1024], P('tm'), may hold values 0 or 1
- readings: float32 [32, 1024], P('tm'), may hold values from -6 to 6
- prior_mean: float32 [1024], replicated, may hold values from -6 to 6
Outputs:
- filtered: float32 [32, 1024], P('tm', 'state')
Inputs may be any that keep to these rules, and one draw needn't show every extreme that they name: `prior_cov`: symmetric and positive definite.
All inputs are finite; a program needn't handle non-finite values. Where the computation divides by a largest or mean magnitude, that divisor is 1e-20 or more. No bound on the sum of `sensor_mask` on one device may be relied on, other than what follows from the above.
Results may differ from a plain program's by a relative error of at most 0.0003.
Values sent between devices are 32-bit elements; how exact they have to be, the bound alone decides.
A program may use at most 64 MiB of HBM per device.

v0:
```python
import jax
import jax.numpy as jnp
from jax import lax
from jax.sharding import PartitionSpec as P

NS_STEPS = 8


HIGHEST = lax.Precision.HIGHEST


def from_behind(value, axis, steps):
    count = lax.axis_size(axis)
    first, last = (max(0, -steps), min(count, count - steps))
    return lax.ppermute(value, axis, [(source, source + steps) for source in range(first, last)])


def matmul(former, latter):
    return jnp.dot(former, latter, precision=HIGHEST, preferred_element_type=jnp.float32)


def per_device(transition, prior_cov, noise_var, sensor_mask, readings, prior_mean):
    states = transition.shape[0]
    row_count = states // lax.axis_size("state")
    first_row = lax.axis_index("state") * row_count
    present = sensor_mask[0].astype(jnp.float32)
    system = present[:, None] * prior_cov * present[None, :] + jnp.diag(noise_var)
    scale_bound = jnp.max(jnp.sum(jnp.abs(system), axis=1))
    identity = jnp.eye(states, dtype=jnp.float32)
    first_iter = 2.0 * identity / scale_bound - system / (scale_bound * scale_bound)
    first_rows = lax.dynamic_slice_in_dim(first_iter, first_row, row_count, 0)
    rows_now = 2.0 * first_rows - matmul(matmul(first_rows, system), first_iter)
    for iteration in range(2, NS_STEPS - 1):
        product_rows = matmul(rows_now, system)

        def absorb_middle(running, portion, anchor, factor=product_rows):
            return matmul(factor, portion)

        folded = absorb_middle(
            jnp.zeros_like(rows_now),
            lax.all_gather(rows_now, "state", axis=0, tiled=True),
            jnp.int32(0),
        )
        rows_now = 2.0 * rows_now - folded
    last_full = lax.all_gather(rows_now, "state", axis=0, tiled=True)
    weighted = lax.dynamic_slice_in_dim(prior_cov, first_row, row_count, 0) * present[None, :]
    projected = matmul(weighted, last_full)
    corrected = 2.0 * projected - matmul(matmul(projected, system), last_full)
    masked_transition = present[:, None] * transition
    own_transition = lax.dynamic_slice_in_dim(transition, first_row, row_count, 0)
    map_part = own_transition - matmul(corrected, masked_transition)
    offset_part = matmul(corrected, present * readings[0])
    position = lax.axis_index("tm")

    def advance_rows(counter, current):
        before = from_behind(current, "tm", 1)
        gathered = lax.all_gather(before, "state", axis=0, tiled=True)
        starting = jnp.where(position == 0, prior_mean, gathered)
        return matmul(map_part, starting) + offset_part

    filtered = lax.fori_loop(0, lax.axis_size("tm"), advance_rows, offset_part)
    return filtered[None, :]


def solution(mesh):
    placed = (P(), P(), P(), P("tm", None), P("tm", None), P())
    return jax.shard_map(
        per_device, mesh=mesh, in_specs=placed, out_specs=P("tm", "state"), check_vma=False
    )
```

profile of v0, /device:TPU:130, one launch (start us, length us, event | category | flops | bytes accessed | tf_op | source)
XLA Modules:
  0.0 1859.2 jit_solution(12972828248887046843)
XLA Ops:
  7.2 4.9 abs_reduce_fusion
  13.9 5.7 divide_subtract_fusion
  19.6 5.1 fusion.10
  24.6 3.4 convolution_subtract_fusion.6
  28.1 4.9 fusion.15
  33.0 65.0 %all-gather.7.cloned.1.call-done = f32[1024,1024]{1,0:T(8,128)} async-done(((f32[64,1024]{1,0:T(8,128)}), f32[1024,1024]{1,0:T(8,128)}) %all-gather.7.cloned.1.call-update) | async-done | bytes 4194320 | tf_op jit(solution)/shard_map/all_gather | solution.py:41
  98.0 5.5 convolution_subtract_fusion.5
  103.9 4.9 fusion.16
  108.8 61.6 %all-gather.9.cloned.1.call-done = f32[1024,1024]{1,0:T(8,128)} async-done(((f32[64,1024]{1,0:T(8,128)}), f32[1024,1024]{1,0:T(8,128)}) %all-gather.9.cloned.1.call-update) | async-done | bytes 4194320 | tf_op jit(solution)/shard_map/all_gather | solution.py:41
  170.4 5.5 convolution_subtract_fusion.4
  176.0 4.9 fusion.17
  180.9 61.8 %all-gather.11.cloned.1.call-done = f32[1024,1024]{1,0:T(8,128)} async-done(((f32[64,1024]{1,0:T(8,128)}), f32[1024,1024]{1,0:T(8,128)}) %all-gather.11.cloned.1.call-update) | async-done | bytes 4194320 | tf_op jit(solution)/shard_map/all_gather | solution.py:41
  242.7 5.5 convolution_subtract_fusion.3
  248.3 4.9 fusion.18
  253.2 61.8 %all-gather.13.cloned.1.call-done = f32[1024,1024]{1,0:T(8,128)} async-done(((f32[64,1024]{1,0:T(8,128)}), f32[1024,1024]{1,0:T(8,128)}) %all-gather.13.cloned.1.call-update) | async-done | bytes 4194320 | tf_op jit(solution)/shard_map/all_gather | solution.py:41
  315.1 5.5 convolution_subtract_fusion.2
  320.6 10.1 all-gather.17.cloned.1.call-start
  330.7 4.9 fusion.19
  335.7 51.7 %all-gather.15.cloned.1.call-done = f32[1024,1024]{1,0:T(8,128)} async-done(((f32[64,1024]{1,0:T(8,128)}), f32[1024,1024]{1,0:T(8,128)}) %all-gather.15.cloned.1.call-update) | async-done | bytes 4194320 | tf_op jit(solution)/shard_map/all_gather | solution.py:41
  387.4 5.5 convolution_subtract_fusion.1
  393.0 66.8 %all-gather.17.cloned.1.call-done = f32[1024,1024]{1,0:T(8,128)} async-done(((f32[64,1024]{1,0:T(8,128)}), f32[1024,1024]{1,0:T(8,128)}) %all-gather.17.cloned.1.call-update) | async-done | bytes 4194320 | tf_op jit(solution)/shard_map/all_gather | solution.py:45
  459.8 5.1 fusion.7
  464.8 2.6 fusion.20
  467.5 2.6 convolution_subtract_fusion
  470.2 2.8 fusion.4
  473.3 1378.3 %while.12 = (s32[]{:T(128)}, f32[64]{0:T(128)S(1)}, pred[]{:T(512)}, f32[1024]{0:T(1024)S(1)}, f32[64,1024]{1,0:T(8,128)S(1)}, /*index=5*/f32[64]{0:T(128)S(1)},...) while((s32[]{:T(128)}, f32[64]{0:T(128)S(1)}, pred[]{:T(512)}, f32[1024]{0:T(1024)S(1)}, ...), condition=%wide.region_3.4_spmd, body=%wide.region_2.3_spmd.sunk | while | flops 788549 | bytes 293070 | solution.py:61
  477.2 2.2 collective-permute-done
  479.6 36.0 %all-reduce.2 = f32[1024]{0:T(1024)S(1)} all-reduce(f32[1024]{0:T(1024)S(1)} %dynamic-update-slice.2), channel_id=1, replica_groups=mesh['tm'=32,'state'=16] {'state'}, use_global_device_ids=true, to_apply=%add | all-reduce | flops 1024 | bytes 8192 | tf_op jit(solution)/shard_map/while
  522.2 38.4 %all-reduce.2 = f32[1024]{0:T(1024)S(1)} all-reduce(f32[1024]{0:T(1024)S(1)} %dynamic-update-slice.2), channel_id=1, replica_groups=mesh['tm'=32,'state'=16] {'state'}, use_global_device_ids=true, to_apply=%add | all-reduce | flops 1024 | bytes 8192 | tf_op jit(solution)/shard_map/while
  567.2 35.4 %all-reduce.2 = f32[1024]{0:T(1024)S(1)} all-reduce(f32[1024]{0:T(1024)S(1)} %dynamic-update-slice.2), channel_id=1, replica_groups=mesh['tm'=32,'state'=16] {'state'}, use_global_device_ids=true, to_apply=%add | all-reduce | flops 1024 | bytes 8192 | tf_op jit(solution)/shard_map/while
  606.8 2.2 collective-permute-done
  609.2 37.4 %all-reduce.2 = f32[1024]{0:T(1024)S(1)} all-reduce(f32[1024]{0:T(1024)S(1)} %dynamic-update-slice.2), channel_id=1, replica_groups=mesh['tm'=32,'state'=16] {'state'}, use_global_device_ids=true, to_apply=%add | all-reduce | flops 1024 | bytes 8192 | tf_op jit(solution)/shard_map/while
  650.8 2.2 collective-permute-done
  653.2 35.4 %all-reduce.2 = f32[1024]{0:T(1024)S(1)} all-reduce(f32[1024]{0:T(1024)S(1)} %dynamic-update-slice.2), channel_id=1, replica_groups=mesh['tm'=32,'state'=16] {'state'}, use_global_device_ids=true, to_apply=%add | all-reduce | flops 1024 | bytes 8192 | tf_op jit(solution)/shard_map/while
  695.2 37.5 %all-reduce.2 = f32[1024]{0:T(1024)S(1)} all-reduce(f32[1024]{0:T(1024)S(1)} %dynamic-update-slice.2), channel_id=1, replica_groups=mesh['tm'=32,'state'=16] {'state'}, use_global_device_ids=true, to_apply=%add | all-reduce | flops 1024 | bytes 8192 | tf_op jit(solution)/shard_map/while
  736.8 2.2 collective-permute-done
  739.3 35.4 %all-reduce.2 = f32[1024]{0:T(1024)S(1)} all-reduce(f32[1024]{0:T(1024)S(1)} %dynamic-update-slice.2), channel_id=1, replica_groups=mesh['tm'=32,'state'=16] {'state'}, use_global_device_ids=true, to_apply=%add | all-reduce | flops 1024 | bytes 8192 | tf_op jit(solution)/shard_map/while
  781.3 37.5 %all-reduce.2 = f32[1024]{0:T(1024)S(1)} all-reduce(f32[1024]{0:T(1024)S(1)} %dynamic-update-slice.2), channel_id=1, replica_groups=mesh['tm'=32,'state'=16] {'state'}, use_global_device_ids=true, to_apply=%add | all-reduce | flops 1024 | bytes 8192 | tf_op jit(solution)/shard_map/while
  822.9 2.2 collective-permute-done
  825.3 35.4 %all-reduce.2 = f32[1024]{0:T(1024)S(1)} all-reduce(f32[1024]{0:T(1024)S(1)} %dynamic-update-slice.2), channel_id=1, replica_groups=mesh['tm'=32,'state'=16] {'state'}, use_global_device_ids=true, to_apply=%add | all-reduce | flops 1024 | bytes 8192 | tf_op jit(solution)/shard_map/while
  867.3 37.5 %all-reduce.2 = f32[1024]{0:T(1024)S(1)} all-reduce(f32[1024]{0:T(1024)S(1)} %dynamic-update-slice.2), channel_id=1, replica_groups=mesh['tm'=32,'state'=16] {'state'}, use_global_device_ids=true, to_apply=%add | all-reduce | flops 1024 | bytes 8192 | tf_op jit(solution)/shard_map/while
  908.9 2.2 collective-permute-done
  911.4 35.4 %all-reduce.2 = f32[1024]{0:T(1024)S(1)} all-reduce(f32[1024]{0:T(1024)S(1)} %dynamic-update-slice.2), channel_id=1, replica_groups=mesh['tm'=32,'state'=16] {'state'}, use_global_device_ids=true, to_apply=%add | all-reduce | flops 1024 | bytes 8192 | tf_op jit(solution)/shard_map/while
  953.4 37.5 %all-reduce.2 = f32[1024]{0:T(1024)S(1)} all-reduce(f32[1024]{0:T(1024)S(1)} %dynamic-update-slice.2), channel_id=1, replica_groups=mesh['tm'=32,'state'=16] {'state'}, use_global_device_ids=true, to_apply=%add | all-reduce | flops 1024 | bytes 8192 | tf_op jit(solution)/shard_map/while
  997.4 35.4 %all-reduce.2 = f32[1024]{0:T(1024)S(1)} all-reduce(f32[1024]{0:T(1024)S(1)} %dynamic-update-slice.2), channel_id=1, replica_groups=mesh['tm'=32,'state'=16] {'state'}, use_global_device_ids=true, to_apply=%add | all-reduce | flops 1024 | bytes 8192 | tf_op jit(solution)/shard_map/while
  1039.4 37.5 %all-reduce.2 = f32[1024]{0:T(1024)S(1)} all-reduce(f32[1024]{0:T(1024)S(1)} %dynamic-update-slice.2), channel_id=1, replica_groups=mesh['tm'=32,'state'=16] {'state'}, use_global_device_ids=true, to_apply=%add | all-reduce | flops 1024 | bytes 8192 | tf_op jit(solution)/shard_map/while
  1083.5 35.4 %all-reduce.2 = f32[1024]{0:T(1024)S(1)} all-reduce(f32[1024]{0:T(1024)S(1)} %dynamic-update-slice.2), channel_id=1, replica_groups=mesh['tm'=32,'state'=16] {'state'}, use_global_device_ids=true, to_apply=%add | all-reduce | flops 1024 | bytes 8192 | tf_op jit(solution)/shard_map/while
  1125.5 37.5 %all-reduce.2 = f32[1024]{0:T(1024)S(1)} all-reduce(f32[1024]{0:T(1024)S(1)} %dynamic-update-slice.2), channel_id=1, replica_groups=mesh['tm'=32,'state'=16] {'state'}, use_global_device_ids=true, to_apply=%add | all-reduce | flops 1024 | bytes 8192 | tf_op jit(solution)/shard_map/while
  1169.5 35.4 %all-reduce.2 = f32[1024]{0:T(1024)S(1)} all-reduce(f32[1024]{0:T(1024)S(1)} %dynamic-update-slice.2), channel_id=1, replica_groups=mesh['tm'=32,'state'=16] {'state'}, use_global_device_ids=true, to_apply=%add | all-reduce | flops 1024 | bytes 8192 | tf_op jit(solution)/shard_map/while
  1211.5 37.5 %all-reduce.2 = f32[1024]{0:T(1024)S(1)} all-reduce(f32[1024]{0:T(1024)S(1)} %dynamic-update-slice.2), channel_id=1, replica_groups=mesh['tm'=32,'state'=16] {'state'}, use_global_device_ids=true, to_apply=%add | all-reduce | flops 1024 | bytes 8192 | tf_op jit(solution)/shard_map/while
  1255.6 35.4 %all-reduce.2 = f32[1024]{0:T(1024)S(1)} all-reduce(f32[1024]{0:T(1024)S(1)} %dynamic-update-slice.2), channel_id=1, replica_groups=mesh['tm'=32,'state'=16] {'state'}, use_global_device_ids=true, to_apply=%add | all-reduce | flops 1024 | bytes 8192 | tf_op jit(solution)/shard_map/while
  1297.6 37.5 %all-reduce.2 = f32[1024]{0:T(1024)S(1)} all-reduce(f32[1024]{0:T(1024)S(1)} %dynamic-update-slice.2), channel_id=1, replica_groups=mesh['tm'=32,'state'=16] {'state'}, use_global_device_ids=true, to_apply=%add | all-reduce | flops 1024 | bytes 8192 | tf_op jit(solution)/shard_map/while
  1341.6 35.4 %all-reduce.2 = f32[1024]{0:T(1024)S(1)} all-reduce(f32[1024]{0:T(1024)S(1)} %dynamic-update-slice.2), channel_id=1, replica_groups=mesh['tm'=32,'state'=16] {'state'}, use_global_device_ids=true, to_apply=%add | all-reduce | flops 1024 | bytes 8192 | tf_op jit(solution)/shard_map/while
  1383.6 37.5 %all-reduce.2 = f32[1024]{0:T(1024)S(1)} all-reduce(f32[1024]{0:T(1024)S(1)} %dynamic-update-slice.2), channel_id=1, replica_groups=mesh['tm'=32,'state'=16] {'state'}, use_global_device_ids=true, to_apply=%add | all-reduce | flops 1024 | bytes 8192 | tf_op jit(solution)/shard_map/while
  1427.7 35.4 %all-reduce.2 = f32[1024]{0:T(1024)S(1)} all-reduce(f32[1024]{0:T(1024)S(1)} %dynamic-update-slice.2), channel_id=1, replica_groups=mesh['tm'=32,'state'=16] {'state'}, use_global_device_ids=true, to_apply=%add | all-reduce | flops 1024 | bytes 8192 | tf_op jit(solution)/shard_map/while
  1469.7 37.5 %all-reduce.2 = f32[1024]{0:T(1024)S(1)} all-reduce(f32[1024]{0:T(1024)S(1)} %dynamic-update-slice.2), channel_id=1, replica_groups=mesh['tm'=32,'state'=16] {'state'}, use_global_device_ids=true, to_apply=%add | all-reduce | flops 1024 | bytes 8192 | tf_op jit(solution)/shard_map/while
  1513.7 35.4 %all-reduce.2 = f32[1024]{0:T(1024)S(1)} all-reduce(f32[1024]{0:T(1024)S(1)} %dynamic-update-slice.2), channel_id=1, replica_groups=mesh['tm'=32,'state'=16] {'state'}, use_global_device_ids=true, to_apply=%add | all-reduce | flops 1024 | bytes 8192 | tf_op jit(solution)/shard_map/while
  1555.7 37.5 %all-reduce.2 = f32[1024]{0:T(1024)S(1)} all-reduce(f32[1024]{0:T(1024)S(1)} %dynamic-update-slice.2), channel_id=1, replica_groups=mesh['tm'=32,'state'=16] {'state'}, use_global_device_ids=true, to_apply=%add | all-reduce | flops 1024 | bytes 8192 | tf_op jit(solution)/shard_map/while
  1599.8 35.4 %all-reduce.2 = f32[1024]{0:T(1024)S(1)} all-reduce(f32[1024]{0:T(1024)S(1)} %dynamic-update-slice.2), channel_id=1, replica_groups=mesh['tm'=32,'state'=16] {'state'}, use_global_device_ids=true, to_apply=%add | all-reduce | flops 1024 | bytes 8192 | tf_op jit(solution)/shard_map/while
  1641.8 37.5 %all-reduce.2 = f32[1024]{0:T(1024)S(1)} all-reduce(f32[1024]{0:T(1024)S(1)} %dynamic-update-slice.2), channel_id=1, replica_groups=mesh['tm'=32,'state'=16] {'state'}, use_global_device_ids=true, to_apply=%add | all-reduce | flops 1024 | bytes 8192 | tf_op jit(solution)/shard_map/while
  1685.8 35.4 %all-reduce.2 = f32[1024]{0:T(1024)S(1)} all-reduce(f32[1024]{0:T(1024)S(1)} %dynamic-update-slice.2), channel_id=1, replica_groups=mesh['tm'=32,'state'=16] {'state'}, use_global_device_ids=true, to_apply=%add | all-reduce | flops 1024 | bytes 8192 | tf_op jit(solution)/shard_map/while
  1727.8 37.5 %all-reduce.2 = f32[1024]{0:T(1024)S(1)} all-reduce(f32[1024]{0:T(1024)S(1)} %dynamic-update-slice.2), channel_id=1, replica_groups=mesh['tm'=32,'state'=16] {'state'}, use_global_device_ids=true, to_apply=%add | all-reduce | flops 1024 | bytes 8192 | tf_op jit(solution)/shard_map/while
  1771.9 35.4 %all-reduce.2 = f32[1024]{0:T(1024)S(1)} all-reduce(f32[1024]{0:T(1024)S(1)} %dynamic-update-slice.2), channel_id=1, replica_groups=mesh['tm'=32,'state'=16] {'state'}, use_global_device_ids=true, to_apply=%add | all-reduce | flops 1024 | bytes 8192 | tf_op jit(solution)/shard_map/while
  1813.9 37.5 %all-reduce.2 = f32[1024]{0:T(1024)S(1)} all-reduce(f32[1024]{0:T(1024)S(1)} %dynamic-update-slice.2), channel_id=1, replica_groups=mesh['tm'=32,'state'=16] {'state'}, use_global_device_ids=true, to_apply=%add | all-reduce | flops 1024 | bytes 8192 | tf_op jit(solution)/shard_map/while
  (258 shorter events, 178.1 us)
Async XLA Ops:
  6.5 91.5 %all-gather.7.cloned.1.call-start = ((), (), s32[]{:S(2)}) async-start(), calls=%async_computation | async-start | bytes 4456448 | tf_op jit(solution)/shard_map/all_gather | solution.py:41
  19.5 5.1 copy-start.1
  28.0 70.0 %copy-start.7 = (f32[64,1024]{1,0:T(8,128)S(1)}, f32[64,1024]{1,0:T(8,128)}, u32[]{:S(2)}) copy-start(f32[64,1024]{1,0:T(8,128)} %convolution_subtract_fusion.6) | copy-start | bytes 786436
  28.0 142.3 %all-gather.9.cloned.1.call-start = ((), (), s32[]{:S(2)}) async-start(), calls=%async_computation.1 | async-start | bytes 4456448 | tf_op jit(solution)/shard_map/all_gather | solution.py:41
  103.5 66.8 %copy-start.3 = (f32[64,1024]{1,0:T(8,128)S(1)}, f32[64,1024]{1,0:T(8,128)}, u32[]{:S(2)}) copy-start(f32[64,1024]{1,0:T(8,128)} %convolution_subtract_fusion.5) | copy-start | bytes 786436
  103.6 139.1 %all-gather.11.cloned.1.call-start = ((), (), s32[]{:S(2)}) async-start(), calls=%async_computation.2 | async-start | bytes 4456448 | tf_op jit(solution)/shard_map/all_gather | solution.py:41
  175.9 66.8 %copy-start.4 = (f32[64,1024]{1,0:T(8,128)S(1)}, f32[64,1024]{1,0:T(8,128)}, u32[]{:S(2)}) copy-start(f32[64,1024]{1,0:T(8,128)} %convolution_subtract_fusion.4) | copy-start | bytes 786436
  175.9 139.1 %all-gather.13.cloned.1.call-start = ((), (), s32[]{:S(2)}) async-start(), calls=%async_computation.3 | async-start | bytes 4456448 | tf_op jit(solution)/shard_map/all_gather | solution.py:41
  248.2 66.8 %copy-start.5 = (f32[64,1024]{1,0:T(8,128)S(1)}, f32[64,1024]{1,0:T(8,128)}, u32[]{:S(2)}) copy-start(f32[64,1024]{1,0:T(8,128)} %convolution_subtract_fusion.3) | copy-start | bytes 786436
  248.3 139.1 %all-gather.15.cloned.1.call-start = ((), (), s32[]{:S(2)}) async-start(), calls=%async_computation.4 | async-start | bytes 4456448 | tf_op jit(solution)/shard_map/all_gather | solution.py:41
  320.6 66.8 %copy-start.6 = (f32[64,1024]{1,0:T(8,128)S(1)}, f32[64,1024]{1,0:T(8,128)}, u32[]{:S(2)}) copy-start(f32[64,1024]{1,0:T(8,128)} %convolution_subtract_fusion.2) | copy-start | bytes 786436
  320.6 72.4 %copy-start.10 = (f32[1,1024]{1,0:T(1,128)S(1)}, f32[1,1024]{1,0:T(1,128)}, u32[]{:S(2)}) copy-start(f32[1,1024]{1,0:T(1,128)} %param.12) | copy-start | bytes 12292
  320.6 139.1 %all-gather.17.cloned.1.call-start = ((), (), s32[]{:S(2)}) async-start(), calls=%async_computation.5 | async-start | bytes 4456448 | tf_op jit(solution)/shard_map/all_gather | solution.py:45
  459.8 5.1 copy-start
  459.8 7.7 copy-start.2
  464.8 5.3 copy-start.8
  467.5 5.8 copy-start.9
  473.3 6.1 collective-permute-start
  515.9 6.1 collective-permute-start
  560.9 6.1 collective-permute-start
  602.9 6.1 collective-permute-start
  646.9 6.1 collective-permute-start
  688.9 6.1 collective-permute-start
  733.0 6.1 collective-permute-start
  775.0 6.1 collective-permute-start
  819.0 6.1 collective-permute-start
  861.0 6.1 collective-permute-start
  905.1 6.1 collective-permute-start
  947.1 6.1 collective-permute-start
  991.1 6.1 collective-permute-start
  1033.1 6.1 collective-permute-start
  1077.2 6.1 collective-permute-start
  1119.2 6.1 collective-permute-start
  1163.2 6.1 collective-permute-start
  1205.2 6.1 collective-permute-start
  1249.3 6.1 collective-permute-start
  1291.3 6.1 collective-permute-start
  1335.3 6.1 collective-permute-start
  1377.3 6.1 collective-permute-start
  1421.4 6.1 collective-permute-start
  1463.4 6.1 collective-permute-start
  1507.4 6.1 collective-permute-start
  1549.4 6.1 collective-permute-start
  1593.5 6.1 collective-permute-start
  1635.5 6.1 collective-permute-start
  1679.5 6.1 collective-permute-start
  1721.5 6.1 collective-permute-start
  1765.6 6.1 collective-permute-start
  1807.6 6.1 collective-permute-start
  1851.6 0.6 copy-start.11
Sparse Core Ops, SparseCore 0:
  28.1 69.8 all-gather.6
  103.7 66.6 all-gather.8
  176.0 66.6 all-gather.10
  248.4 66.6 all-gather.12
  320.7 66.6 all-gather.14
  393.1 66.6 all-gather.16
where the time goes:
time: 1870 us; the launch traced here: 1860 us
  blocking collectives  1170 us (63%)
  waiting for transfers between devices  440 us (24%)
  matrix products  82.4 us (4%)
  starting transfers between devices  72.9 us (4%)
  local copies, waits for them, and re-layouts  47.2 us (3%)
  loops' own time  21.6 us (1%)
    while x32, blocking collectives  1170 us
    all_gather x5, waiting for transfers between devices, per_device(): lax.all_gather(rows_now, 'state', axis=0, tiled=True)  302 us
    dot_general x49, matrix products, matmul(): jnp.dot(former, latter, precision=HIGHEST, preferred_element_type=jnp.flo...  82.4 us
    ppermute x32, waiting for transfers between devices, from_behind(): lax.ppermute(value, axis, [(source, source + steps) for source in range(f...  71.3 us
    all_gather x1, waiting for transfers between devices, per_device(): last_full = lax.all_gather(rows_now, 'state', axis=0, tiled=True)  66.8 us
    ppermute x32, starting transfers between devices, from_behind(): lax.ppermute(value, axis, [(source, source + steps) for source in range(f...  62.4 us
    while x96, local copies, waits for them, and re-layouts  46.6 us
  transfers between devices with their start and end apart: 38, of which 38 were waited for; matrix products, arithmetic and copies ran while one was open for 4% of the time, Pallas kernels for 0%

commit v1 on v0

v1 whole, which is shorter than its diff:
```python
import functools
import jax
import jax.numpy as jnp
from jax import lax
from jax.experimental import pallas as pl
from jax.experimental.pallas import tpu as pltpu
from jax.sharding import PartitionSpec as P

f32 = jnp.float32
bf16 = jnp.bfloat16
S = 1024
BLK = 256
LANE = 128
SQUARINGS = 7
T_SLOT, P_SLOT, Y_SLOT = 8, 9, 10
W_SLOT, M_SLOT, OTHER_SLOT = 0, 1, 7

PRODUCT_FROM = (1, 2, 2, 3, 3, 4, 5)
MAP_FROM = 8
SHIP_FROM = 9
MESH_ID = pl.DeviceIdType.MESH


def split(value):
    high = value.astype(bf16)
    return high, (value - high.astype(f32)).astype(bf16)


def dot(left, right):
    return jnp.dot(left, right, preferred_element_type=f32)


def dot3(left_high, left_low, right_high, right_low):
    return dot(left_high, right_high) + dot(left_high, right_low) + dot(left_low, right_high)


def matvec(mats, slot, x):
    parts = []
    for i in range(S // LANE):
        total = None
        for k in range(S // LANE):
            tile = mats[slot, pl.ds(i * LANE, LANE), pl.ds(k * LANE, LANE)]
            term = tile * x[:, k * LANE:(k + 1) * LANE]
            total = term if total is None else total + term
        parts.append(jnp.sum(total.T, axis=0, keepdims=True))
    return jnp.concatenate(parts, axis=1)


def mirror(mats, slot):
    for i in range(S // BLK):
        for j in range(i):
            rows, cols = pl.ds(i * BLK, BLK), pl.ds(j * BLK, BLK)
            mats[slot, rows, cols] = mats[slot, cols, rows].T


def split_into(mats, slot, high, low):
    for i in range(S // BLK):
        rows = pl.ds(i * BLK, BLK)
        high[rows, :], low[rows, :] = split(mats[slot, rows, :])


def upper_step(mats, source, target, lh, ll, rh, rl):
    for i in range(S // BLK):
        rows, cols = pl.ds(i * BLK, BLK), pl.ds(i * BLK, S - i * BLK)
        product = dot3(lh[rows, :], ll[rows, :], rh[:, cols], rl[:, cols])
        mats[target, rows, cols] = 2.0 * mats[source, rows, cols] - product
    mirror(mats, target)


def kernel(planes, t_hbm, p_hbm, noise_ref, mask_ref, read_ref, mean_ref, out_ref,
           mats, gh, gl, yh, yl, offset, other_offset, xin, xmid, xout, yvec, bound,
           load_sem, send_sem, recv_sem, ready_sem):
    tm = lax.axis_index("tm")
    state = lax.axis_index("state")
    z, core = lax.div(tm, 2), lax.rem(tm, 2)
    products = sum((z >= first).astype(jnp.int32) for first in PRODUCT_FROM)
    has_map = z >= MAP_FROM
    ships = z >= SHIP_FROM
    entry_core = ships.astype(jnp.int32)
    next_entry = (z + 1 >= SHIP_FROM).astype(jnp.int32)
    has_next = jnp.logical_and(core == 1, z < planes - 1)
    has_before = jnp.logical_and(core == entry_core, z > 0)

    barrier = pltpu.get_barrier_semaphore()

    def greet(where):
        pl.semaphore_signal(barrier, inc=1, device_id=(where, state), device_id_type=MESH_ID)

    partner = z * 2 + 1 - core
    following = (z + 1) * 2 + next_entry
    greet(partner)

    @pl.when(has_next)
    def _():
        greet(following)

    @pl.when(has_before)
    def _():
        greet((z - 1) * 2 + 1)

    load_p = pltpu.make_async_copy(p_hbm, mats.at[P_SLOT], load_sem.at[0])
    load_t = pltpu.make_async_copy(t_hbm, mats.at[T_SLOT], load_sem.at[1])
    load_p.start()
    load_t.start()

    present = mask_ref[...].astype(f32)
    observed = present * read_ref[...]
    row_id = lax.broadcasted_iota(jnp.int32, (LANE, LANE), 0)
    col_id = lax.broadcasted_iota(jnp.int32, (LANE, LANE), 1)
    on_diagonal = row_id == col_id

    load_p.wait()
    sums = [jnp.zeros((8, LANE), f32) for _ in range(S // LANE)]
    for i in range(S // LANE):
        rows = pl.ds(i * LANE, LANE)
        down = jnp.broadcast_to(present[:, i * LANE:(i + 1) * LANE], (LANE, LANE)).T
        for k in range(S // LANE):
            cols = pl.ds(k * LANE, LANE)
            tile = mats[P_SLOT, rows, cols] * present[:, k * LANE:(k + 1) * LANE] * down
            if i == k:
                tile = tile + jnp.where(on_diagonal, noise_ref[:, cols], 0.0)
            mats[0, rows, cols] = tile
            sums[k] = sums[k] + jnp.sum(jnp.abs(tile).reshape(LANE // 8, 8, LANE), axis=0)
    row_sums = jnp.concatenate([jnp.sum(part, axis=0, keepdims=True) for part in sums], axis=1)
    inverse_bound = 1.0 / jnp.max(row_sums, axis=1, keepdims=True)
    bound[...] = jnp.broadcast_to(inverse_bound, (1, LANE))
    for i in range(S // BLK):
        rows = pl.ds(i * BLK, BLK)
        scaled = mats[0, rows, :] * inverse_bound
        mats[0, rows, :] = scaled
        gh[rows, :], gl[rows, :] = split(scaled)

    def square(j, carry):
        upper_step(mats, j, j + 1, gh, gl, gh, gl)
        split_into(mats, j + 1, gh, gl)
        return carry

    lax.fori_loop(0, SQUARINGS, square, 0)

    @pl.when(products > 0)
    def _():
        scale = bound[:, :1]
        for i in range(S // LANE):
            rows = pl.ds(i * LANE, LANE)
            for k in range(S // LANE):
                cols = pl.ds(k * LANE, LANE)
                tile = -mats[0, rows, cols]
                if i == k:
                    tile = tile + jnp.where(on_diagonal, 2.0, 0.0)
                tile = tile * scale
                mats[Y_SLOT, rows, cols] = tile
                yh[rows, cols], yl[rows, cols] = split(tile)

    def multiply(q, carry):
        split_into(mats, q, gh, gl)
        upper_step(mats, Y_SLOT, Y_SLOT, yh, yl, gh, gl)
        split_into(mats, Y_SLOT, yh, yl)
        return carry

    lax.fori_loop(1, products + 1, multiply, 0)

    load_t.wait()

    @pl.when(has_map)
    def _():
        for i in range(S // BLK):
            rows = pl.ds(i * BLK, BLK)
            gh[rows, :], gl[rows, :] = split(mats[P_SLOT, rows, :] * present)
        for i in range(S // BLK):
            rows = pl.ds(i * BLK, BLK)
            mats[W_SLOT, rows, :] = dot3(gh[rows, :], gl[rows, :], yh[...], yl[...])
        offset[...] = matvec(mats, W_SLOT, observed)
        for i in range(S // BLK):
            rows = pl.ds(i * BLK, BLK)
            gh[rows, :], gl[rows, :] = split(mats[W_SLOT, rows, :] * present)
            yh[rows, :], yl[rows, :] = split(mats[T_SLOT, rows, :])
        for i in range(S // BLK):
            rows = pl.ds(i * BLK, BLK)
            mats[M_SLOT, rows, :] = mats[T_SLOT, rows, :] - dot3(gh[rows, :], gl[rows, :], yh[...], yl[...])

    pl.semaphore_wait(barrier, 1 + has_next.astype(jnp.int32) + has_before.astype(jnp.int32))

    def send(source, target, index, where):
        return pltpu.make_async_remote_copy(
            src_ref=source, dst_ref=target, send_sem=send_sem.at[index], recv_sem=recv_sem.at[index],
            device_id=(where, state), device_id_type=MESH_ID)

    mean_in = send(xout, xin, 0, following)
    map_over = send(mats.at[M_SLOT], mats.at[OTHER_SLOT], 1, partner)
    offset_over = send(offset, other_offset, 2, partner)

    @pl.when(jnp.logical_and(ships, core == 1))
    def _():
        pl.semaphore_signal(ready_sem, inc=1, device_id=(partner, state), device_id_type=MESH_ID)

    @pl.when(jnp.logical_and(ships, core == 0))
    def _():
        pl.semaphore_wait(ready_sem, 1)
        map_over.start()
        offset_over.start()

    @pl.when(jnp.logical_and(ships, core == 1))
    def _():
        map_over.wait_recv()
        offset_over.wait_recv()

    @pl.when(tm == 0)
    def _():
        xin[...] = mean_ref[...]

    @pl.when(tm > 0)
    def _():
        mean_in.wait_recv()

    middle_out = send(xmid, xin, 0, partner)

    @pl.when(jnp.logical_not(ships))
    def _():
        @pl.when(has_map)
        def _():
            xout[...] = matvec(mats, M_SLOT, xin[...]) + offset[...]

        @pl.when(jnp.logical_not(has_map))
        def _():
            moved = matvec(mats, T_SLOT, xin[...])
            gap = observed - present * moved

            @pl.when(products == 0)
            def _():
                yvec[...] = gap * bound[:, :1]

            @pl.when(products > 0)
            def _():
                yvec[...] = matvec(mats, Y_SLOT, gap)

            def apply(j, carry):
                y = yvec[...]
                yvec[...] = 2.0 * y - matvec(mats, j, y)
                return carry

            lax.fori_loop(jnp.where(products == 0, 0, products + 1), SQUARINGS + 1, apply, 0)
            xout[...] = moved + matvec(mats, P_SLOT, present * yvec[...])

    @pl.when(jnp.logical_and(ships, core == 1))
    def _():
        middle = matvec(mats, OTHER_SLOT, xin[...]) + other_offset[...]
        xmid[...] = middle
        middle_out.start()
        xout[...] = matvec(mats, M_SLOT, middle) + offset[...]

    @pl.when(jnp.logical_and(ships, core == 0))
    def _():
        xout[...] = xin[...]

    inner_out = send(xout, xin, 0, partner)
    inner = jnp.logical_and(jnp.logical_not(ships), core == 0)

    @pl.when(inner)
    def _():
        inner_out.start()

    @pl.when(has_next)
    def _():
        mean_in.start()

    out_ref[...] = xout[...]

    @pl.when(inner)
    def _():
        inner_out.wait_send()

    @pl.when(has_next)
    def _():
        mean_in.wait_send()

    @pl.when(jnp.logical_and(ships, core == 0))
    def _():
        map_over.wait_send()
        offset_over.wait_send()

    @pl.when(jnp.logical_and(ships, core == 1))
    def _():
        middle_out.wait_send()


def per_device(transition, prior_cov, noise_var, sensor_mask, readings, prior_mean):
    planes = lax.axis_size("tm") // 2
    row = lambda value: value.reshape(1, S)
    vmem = pl.BlockSpec(memory_space=pltpu.VMEM)
    hbm = pl.BlockSpec(memory_space=pl.ANY)
    vector = pltpu.VMEM((1, S), f32)
    half = pltpu.VMEM((S, S), bf16)
    mean = pl.pallas_call(
        functools.partial(kernel, planes),
        out_shape=jax.ShapeDtypeStruct((1, S), f32),
        in_specs=[hbm, hbm, vmem, vmem, vmem, vmem],
        out_specs=vmem,
        scratch_shapes=[
            pltpu.VMEM((11, S, S), f32), half, half, half, half,
            vector, vector, vector, vector, vector, vector, pltpu.VMEM((1, LANE), f32),
            pltpu.SemaphoreType.DMA((2,)), pltpu.SemaphoreType.DMA((3,)), pltpu.SemaphoreType.DMA((3,)),
            pltpu.SemaphoreType.REGULAR,
        ],
        compiler_params=pltpu.CompilerParams(
            collective_id=0, has_side_effects=True, vmem_limit_bytes=63 * 2 ** 20),
    )(transition, prior_cov, row(noise_var), sensor_mask, readings, row(prior_mean))
    share = S // lax.axis_size("state")
    return lax.dynamic_slice_in_dim(mean, lax.axis_index("state") * share, share, 1)


def solution(mesh):
    placed = (P(), P(), P(), P("tm", None), P("tm", None), P())
    return jax.shard_map(
        per_device, mesh=mesh, in_specs=placed, out_specs=P("tm", "state"), check_vma=False
    )
```

time: 1870 us -> 116 us (0.06)
  the two profiles are of different devices: /device:TPU:130 before, /device:TPU:481 now
where the time goes in v1:
time: 116 us
  Pallas kernels  114 us (98%)
  local copies, waits for them, and re-layouts  1.27 us (1%)
    pallas_call x1, Pallas kernels, per_device(): pl.pallas_call(functools.partial(kernel, planes), out_shape=jax.ShapeDtyp...  114 us

profile of v1, /device:TPU:481, one launch (start us, length us, event | category | flops | bytes accessed | tf_op | source)
XLA Modules:
  0.0 115.5 jit_solution(4220338486296843455)
XLA Ops:
  0.0 114.3 %shard_map.64 = f32[1,1024]{1,0:T(1,128)} custom-call(f32[1024,1024]{1,0:T(8,128)} %t_hbm.1, f32[1024,1024]{1,0:T(8,128)} %p_hbm.1, f32[1,1024]{1,0:T(1,128)} %bitcast.2, s32[1,1024]{1,0:T(1,128)} %mask_ref.1, f32[1,1024]{1,0:T(1,128)} %read_ref.1, f32[1,1024]{1,0:T(1,128)} %bitcast.3), custom_call_target="tpu_custom_call" | custom-call | tf_op jit(solution)/shard_map/pallas_call | solution.py:293
  114.3 1.3 %constant_dynamic-slice_fusion = f32[1,64]{1,0:T(1,128)} fusion(f32[1,1024]{1,0:T(1,128)} %shard_map.64, s32[]{:T(128)S(6)} %select_n.3), kind=kLoop, calls=%fused_computation | loop fusion | bytes 516 | tf_op jit(solution)/shard_map/dynamic_slice | solution.py:308

commit v2 on v1

v2 whole, which is shorter than its diff:
```python
import functools
import jax
import jax.numpy as jnp
from jax import lax
from jax.experimental import pallas as pl
from jax.experimental.pallas import tpu as pltpu
from jax.sharding import PartitionSpec as P

f32 = jnp.float32
bf16 = jnp.bfloat16
S = 1024
BLK = 256
LANE = 128
WIDE = 512
SQUARINGS = 7
FIRST_TOPS = (4, 5)
T_SLOT, P_SLOT = 8, 9
W_SLOT, M_SLOT, OTHER_SLOT = 0, 1, 7

PRODUCT_FROM = (2, 3, 3, 4, 4, 5, 5)
GAIN_FROM = 7
MAP_FROM = 9
SHIP_FROM = 9
MESH_ID = pl.DeviceIdType.MESH


def split(value):
    high = value.astype(bf16)
    return high, (value - high.astype(f32)).astype(bf16)


def dot(left, right):
    return jnp.dot(left, right, preferred_element_type=f32)


def dot3(left_high, left_low, right_high, right_low):
    return dot(left_high, right_high) + dot(left_high, right_low) + dot(left_low, right_high)


def matvec(mats, slot, x):
    parts = []
    for i in range(S // LANE):
        total = None
        for k in range(S // LANE):
            tile = mats[slot, pl.ds(i * LANE, LANE), pl.ds(k * LANE, LANE)]
            term = tile * x[:, k * LANE:(k + 1) * LANE]
            total = term if total is None else total + term
        parts.append(jnp.sum(total.T, axis=0, keepdims=True))
    return jnp.concatenate(parts, axis=1)


def column_parts(start, stop):
    return [pl.ds(at, min(WIDE, stop - at)) for at in range(start, stop, WIDE)]


def square(mats, source, target, gh, gl, now):
    later = 1 - now
    for i in range(S // BLK):
        rows = pl.ds(i * BLK, BLK)
        left = gh[now, rows, :]
        for j in range(i + 1, S // BLK):
            cols = pl.ds(j * BLK, BLK)
            mats[target, cols, rows] = dot(left, gl[now, :, cols]).T
        for cols in column_parts(0, i * BLK):
            product = dot(left, gh[now, :, cols]) + dot(left, gl[now, :, cols])
            new = 2.0 * mats[source, rows, cols] - product - mats[target, rows, cols]
            mats[target, rows, cols] = new
            gh[later, rows, cols], gl[later, rows, cols] = split(new)
        cross = dot(left, gl[now, :, rows])
        new = 2.0 * mats[source, rows, rows] - dot(left, gh[now, :, rows]) - (cross + cross.T)
        mats[target, rows, rows] = new
        gh[later, rows, rows], gl[later, rows, rows] = split(new)
        for j in range(i):
            cols = pl.ds(j * BLK, BLK)
            turned = mats[target, rows, cols].T
            mats[target, cols, rows] = turned
            gh[later, cols, rows], gl[later, cols, rows] = split(turned)


def multiply(whole, yh, yl, gh, gl, now):
    for i in range(S // BLK):
        rows = pl.ds(i * BLK, BLK)
        left_high, left_low = yh[rows, :], yl[rows, :]
        for cols in column_parts(0, (i + 1) * BLK):
            product = dot3(left_high, left_low, gh[now, :, cols], gl[now, :, cols])
            new = 2.0 * whole[0, rows, cols] - product
            whole[0, rows, cols] = new
        span = pl.ds(0, (i + 1) * BLK)
        yh[rows, span], yl[rows, span] = split(whole[0, rows, span])
        for j in range(i):
            other = pl.ds(j * BLK, BLK)
            turned = whole[0, rows, other].T
            whole[0, other, rows] = turned
            yh[other, rows], yl[other, rows] = split(turned)


def kernel(planes, t_hbm, p_hbm, noise_ref, mask_ref, read_ref, mean_ref, out_ref,
           mats, whole, gh, gl, yh, yl, offset, other_offset, xin, xmid, xout, xcur, ybase, bound,
           load_sem, send_sem, recv_sem, ready_sem):
    tm = lax.axis_index("tm")
    state = lax.axis_index("state")
    z, core = lax.div(tm, 2), lax.rem(tm, 2)
    products = sum((z >= first).astype(jnp.int32) for first in PRODUCT_FROM)
    late = products == SQUARINGS
    top = jnp.where(tm == 0, FIRST_TOPS[0], jnp.where(tm == 1, FIRST_TOPS[1], SQUARINGS))
    series = jnp.where(tm == 0, 2 ** (SQUARINGS + 1 - FIRST_TOPS[0]) - 1,
                       jnp.where(tm == 1, 2 ** (SQUARINGS + 1 - FIRST_TOPS[1]) - 1, 1))
    series = jnp.where(late, 0, series)
    has_gain = z >= GAIN_FROM
    has_map = z >= MAP_FROM
    ships = z >= SHIP_FROM
    entry_core = ships.astype(jnp.int32)
    next_entry = (z + 1 >= SHIP_FROM).astype(jnp.int32)
    has_next = jnp.logical_and(core == 1, z < planes - 1)
    has_before = jnp.logical_and(core == entry_core, z > 0)

    barrier = pltpu.get_barrier_semaphore()

    def greet(where):
        pl.semaphore_signal(barrier, inc=1, device_id=(where, state), device_id_type=MESH_ID)

    partner = z * 2 + 1 - core
    following = (z + 1) * 2 + next_entry
    greet(partner)

    @pl.when(has_next)
    def _():
        greet(following)

    @pl.when(has_before)
    def _():
        greet((z - 1) * 2 + 1)

    def band(i):
        return pl.ds(pl.multiple_of(i * LANE, LANE), LANE)

    def load_p(i):
        return pltpu.make_async_copy(p_hbm.at[band(i), :], mats.at[P_SLOT, band(i), :], load_sem.at[i])

    def start_load(i, carry):
        load_p(i).start()
        return carry

    bands = S // LANE
    lax.fori_loop(0, bands, start_load, 0)
    load_t = pltpu.make_async_copy(t_hbm, mats.at[T_SLOT], load_sem.at[bands])

    present = mask_ref[...].astype(f32)
    observed = present * read_ref[...]
    row_id = lax.broadcasted_iota(jnp.int32, (LANE, LANE), 0)
    col_id = lax.broadcasted_iota(jnp.int32, (LANE, LANE), 1)
    on_diagonal = row_id == col_id

    def present_down(i):
        down = jnp.broadcast_to(mask_ref[:, band(i)].astype(f32), (LANE, LANE)).T
        return jnp.concatenate([down] * bands, axis=1)

    def add_bands(pair, sums):
        for i in (2 * pair, 2 * pair + 1):
            load_p(i).wait()
        for i in (2 * pair, 2 * pair + 1):
            tile = jnp.abs(mats[P_SLOT, band(i), :]) * present_down(i)
            sums = sums + jnp.sum(tile.reshape(LANE // 8, 8, S), axis=0)
        return sums

    column_sums = jnp.sum(lax.fori_loop(0, bands // 2, add_bands, jnp.zeros((8, S), f32)), axis=0, keepdims=True)
    load_t.start()
    row_sums = present * column_sums + noise_ref[...]
    inverse_bound = 1.0 / jnp.max(row_sums, axis=1, keepdims=True)
    bound[...] = jnp.broadcast_to(inverse_bound, (1, LANE))

    def scale_bands(pair, carry):
        for i in (2 * pair, 2 * pair + 1):
            rows = band(i)
            across = present * bound[:, :1]
            tile = mats[P_SLOT, rows, :] * across * present_down(i)
            mats[0, rows, :] = tile
            gh[0, rows, :], gl[0, rows, :] = split(tile)
        for i in (2 * pair, 2 * pair + 1):
            rows = band(i)
            tile = mats[0, rows, rows] + jnp.where(on_diagonal, noise_ref[:, rows] * bound[...], 0.0)
            mats[0, rows, rows] = tile
            gh[0, rows, rows], gl[0, rows, rows] = split(tile)
        return carry

    lax.fori_loop(0, bands // 2, scale_bands, 0)

    @pl.when(products > 0)
    def _():
        def first_band(i, carry):
            rows = band(i)
            whole[0, rows, :] = mats[0, rows, :] * -bound[:, :1]
            tile = whole[0, rows, rows] + jnp.where(on_diagonal, 2.0 * bound[...], 0.0)
            whole[0, rows, rows] = tile
            yh[rows, :], yl[rows, :] = split(whole[0, rows, :])
            return carry

        lax.fori_loop(0, bands, first_band, 0)

    def two_squarings(pair, carry):
        @pl.when(jnp.logical_and(late, pair > 0))
        def _():
            multiply(whole, yh, yl, gh, gl, 0)

        @pl.when(2 * pair < top)
        def _():
            square(mats, 2 * pair, 2 * pair + 1, gh, gl, 0)

        @pl.when(late)
        def _():
            multiply(whole, yh, yl, gh, gl, 1)

        @pl.when(2 * pair + 1 < top)
        def _():
            square(mats, 2 * pair + 1, 2 * pair + 2, gh, gl, 1)

        return carry

    lax.fori_loop(0, lax.div(top + 1, 2), two_squarings, 0)

    def one_product(q, carry):
        def halve(i, inside):
            gh[0, band(i), :], gl[0, band(i), :] = split(mats[q, band(i), :])
            return inside

        lax.fori_loop(0, bands, halve, 0)
        multiply(whole, yh, yl, gh, gl, 0)
        return carry

    lax.fori_loop(1, jnp.where(late, 1, products + 1), one_product, 0)

    load_t.wait()

    pl.semaphore_wait(barrier, 1 + has_next.astype(jnp.int32) + has_before.astype(jnp.int32))

    def send(source, target, index, where):
        return pltpu.make_async_remote_copy(
            src_ref=source, dst_ref=target, send_sem=send_sem.at[index], recv_sem=recv_sem.at[index],
            device_id=(where, state), device_id_type=MESH_ID)

    mean_in = send(xout, xin, 0, following)
    map_over = send(mats.at[M_SLOT], mats.at[OTHER_SLOT], 1, partner)
    offset_over = send(offset, other_offset, 2, partner)
    hands = jnp.logical_and(ships, core == 0)
    takes = jnp.logical_and(ships, core == 1)

    @pl.when(takes)
    def _():
        pl.semaphore_signal(ready_sem, inc=1, device_id=(partner, state), device_id_type=MESH_ID)

    @pl.when(hands)
    def _():
        pl.semaphore_wait(ready_sem, 1)

    def block(i):
        return pl.ds(pl.multiple_of(i * BLK, BLK), BLK)

    @pl.when(has_gain)
    def _():
        def gain_rows(i, carry):
            rows = block(i)
            left_high, left_low = split(mats[P_SLOT, rows, :] * present)
            for cols in column_parts(0, S):
                mats[W_SLOT, rows, cols] = dot3(left_high, left_low, yh[:, cols], yl[:, cols])
            gh[1, rows, :], gl[1, rows, :] = split(mats[W_SLOT, rows, :] * present)
            gh[0, rows, :], gl[0, rows, :] = split(mats[T_SLOT, rows, :])
            return carry

        lax.fori_loop(0, S // BLK, gain_rows, 0)

    @pl.when(has_map)
    def _():
        offset[...] = matvec(mats, W_SLOT, observed)

        @pl.when(hands)
        def _():
            offset_over.start()

        def map_rows(i, carry):
            rows = block(i)
            for cols in column_parts(0, S):
                mats[M_SLOT, rows, cols] = mats[T_SLOT, rows, cols] - dot3(
                    gh[1, rows, :], gl[1, rows, :], gh[0, :, cols], gl[0, :, cols])

            @pl.when(hands)
            def _():
                send(mats.at[M_SLOT, rows, :], mats.at[OTHER_SLOT, rows, :], 1, partner).start()

            return carry

        lax.fori_loop(0, S // BLK, map_rows, 0)

    @pl.when(takes)
    def _():
        map_over.wait_recv()
        offset_over.wait_recv()

    middle_out = send(xmid, xin, 0, partner)
    inner_out = send(xout, xin, 0, partner)
    inner = jnp.logical_and(jnp.logical_not(ships), core == 0)
    low = jnp.where(products == 0, 0, products + 1)

    @pl.when(tm == 0)
    def _():
        xin[...] = mean_ref[...]

    @pl.when(tm > 0)
    def _():
        mean_in.wait_recv()

    @pl.when(jnp.logical_not(has_gain))
    def _():
        moved = matvec(mats, T_SLOT, xin[...])
        gap = observed - present * moved

        @pl.when(products == 0)
        def _():
            xcur[...] = gap * bound[:, :1]

        @pl.when(products > 0)
        def _():
            xcur[...] = matvec(whole, 0, gap)

        factors = jnp.maximum(top - low, 0)

        def apply(j, y):
            return 2.0 * y - matvec(mats, j, y)

        @pl.when(lax.rem(factors, 2) == 1)
        def _():
            xcur[...] = apply(low, xcur[...])

        def apply_two(pair, carry):
            j = top - 2 - 2 * pair
            xcur[...] = apply(j, apply(j + 1, xcur[...]))
            return carry

        lax.fori_loop(0, lax.div(factors, 2), apply_two, 0)
        ybase[...] = xcur[...]

        def add_power(y):
            return ybase[...] + (y - matvec(mats, top, y))

        @pl.when(series > 0)
        def _():
            xcur[...] = add_power(xcur[...])

        def add_two(step, carry):
            xcur[...] = add_power(add_power(xcur[...]))
            return carry

        lax.fori_loop(0, lax.div(series, 2), add_two, 0)
        xout[...] = moved + matvec(mats, P_SLOT, present * xcur[...])

    @pl.when(jnp.logical_and(has_gain, jnp.logical_not(has_map)))
    def _():
        moved = matvec(mats, T_SLOT, xin[...])
        xout[...] = moved + matvec(mats, W_SLOT, observed - present * moved)

    @pl.when(jnp.logical_and(has_map, jnp.logical_not(ships)))
    def _():
        xout[...] = matvec(mats, M_SLOT, xin[...]) + offset[...]

    @pl.when(takes)
    def _():
        middle = matvec(mats, OTHER_SLOT, xin[...]) + other_offset[...]
        xmid[...] = middle
        xout[...] = matvec(mats, M_SLOT, middle) + offset[...]

        @pl.when(has_next)
        def _():
            mean_in.start()

        middle_out.start()

    @pl.when(inner)
    def _():
        inner_out.start()

    @pl.when(jnp.logical_and(has_next, jnp.logical_not(ships)))
    def _():
        mean_in.start()

    @pl.when(hands)
    def _():
        xout[...] = xin[...]

    out_ref[...] = xout[...]

    @pl.when(inner)
    def _():
        inner_out.wait_send()

    @pl.when(has_next)
    def _():
        mean_in.wait_send()

    @pl.when(hands)
    def _():
        map_over.wait_send()
        offset_over.wait_send()

    @pl.when(takes)
    def _():
        middle_out.wait_send()


def per_device(transition, prior_cov, noise_var, sensor_mask, readings, prior_mean):
    planes = lax.axis_size("tm") // 2
    row = lambda value: value.reshape(1, S)
    vmem = pl.BlockSpec(memory_space=pltpu.VMEM)
    hbm = pl.BlockSpec(memory_space=pl.ANY)
    vector = pltpu.VMEM((1, S), f32)
    half, halves = pltpu.VMEM((S, S), bf16), pltpu.VMEM((2, S, S), bf16)
    mean = pl.pallas_call(
        functools.partial(kernel, planes),
        out_shape=jax.ShapeDtypeStruct((1, S), f32),
        in_specs=[hbm, hbm, vmem, vmem, vmem, vmem],
        out_specs=vmem,
        scratch_shapes=[
            pltpu.VMEM((10, S, S), f32), pltpu.VMEM((1, S, S), f32), halves, halves, half, half,
            *[vector] * 7, pltpu.VMEM((1, LANE), f32),
            pltpu.SemaphoreType.DMA((S // LANE + 1,)), pltpu.SemaphoreType.DMA((3,)), pltpu.SemaphoreType.DMA((3,)),
            pltpu.SemaphoreType.REGULAR,
        ],
        compiler_params=pltpu.CompilerParams(
            collective_id=0, has_side_effects=True, vmem_limit_bytes=63 * 2 ** 20),
    )(transition, prior_cov, row(noise_var), sensor_mask, readings, row(prior_mean))
    share = S // lax.axis_size("state")
    return lax.dynamic_slice_in_dim(mean, lax.axis_index("state") * share, share, 1)


def solution(mesh):
    placed = (P(), P(), P(), P("tm", None), P("tm", None), P())
    return jax.shard_map(
        per_device, mesh=mesh, in_specs=placed, out_specs=P("tm", "state"), check_vma=False
    )
```

time: 116 us -> 109 us (0.940)
  Pallas kernels: 114 us -> 108 us
    pallas_call x1, Pallas kernels: 114 us -> 108 us  [per_device(): pl.pallas_call(functools.partial(kernel, planes), out_shape=jax.ShapeDtyp...]
where the time goes in v2:
time: 109 us
  Pallas kernels  108 us (99%)
  local copies, waits for them, and re-layouts  1.27 us (1%)
    pallas_call x1, Pallas kernels, per_device(): pl.pallas_call(functools.partial(kernel, planes), out_shape=jax.ShapeDtyp...  108 us

profile of v2, /device:TPU:481, one launch (start us, length us, event | category | flops | bytes accessed | tf_op | source)
XLA Modules:
  0.0 109.0 jit_solution(5484847873352415371)
XLA Ops:
  0.0 107.7 %shard_map.64 = f32[1,1024]{1,0:T(1,128)} custom-call(f32[1024,1024]{1,0:T(8,128)} %t_hbm.1, f32[1024,1024]{1,0:T(8,128)} %p_hbm.1, f32[1,1024]{1,0:T(1,128)} %bitcast.2, s32[1,1024]{1,0:T(1,128)} %mask_ref.1, f32[1,1024]{1,0:T(1,128)} %read_ref.1, f32[1,1024]{1,0:T(1,128)} %bitcast.3), custom_call_target="tpu_custom_call" | custom-call | tf_op jit(solution)/shard_map/pallas_call | solution.py:415
  107.7 1.3 %constant_dynamic-slice_fusion = f32[1,64]{1,0:T(1,128)} fusion(f32[1,1024]{1,0:T(1,128)} %shard_map.64, s32[]{:T(128)S(6)} %select_n.3), kind=kLoop, calls=%fused_computation | loop fusion | bytes 516 | tf_op jit(solution)/shard_map/dynamic_slice | solution.py:430

commit v3 on v2

--- a/solution.py
+++ b/solution.py
@@ -13,14 +13,14 @@
 LANE = 128
 WIDE = 512
 SQUARINGS = 7
-FIRST_TOPS = (4, 5)
+FIRST_TOPS = (4, 6)
 T_SLOT, P_SLOT = 8, 9
 W_SLOT, M_SLOT, OTHER_SLOT = 0, 1, 7
 
-PRODUCT_FROM = (2, 3, 3, 4, 4, 5, 5)
+PRODUCT_FROM = (2, 2, 3, 3, 4, 5, 5)
 GAIN_FROM = 7
-MAP_FROM = 9
-SHIP_FROM = 9
+MAP_FROM = 10
+SHIP_FROM = 7
 MESH_ID = pl.DeviceIdType.MESH
 
 
@@ -95,7 +95,7 @@
 
 
 def kernel(planes, t_hbm, p_hbm, noise_ref, mask_ref, read_ref, mean_ref, out_ref,
-           mats, whole, gh, gl, yh, yl, offset, other_offset, xin, xmid, xout, xcur, ybase, bound,
+           mats, whole, gh, gl, yh, yl, offset, other_offset, seen, other_seen, xin, xmid, xout, xcur, ybase, bound,
            load_sem, send_sem, recv_sem, ready_sem):
     tm = lax.axis_index("tm")
     state = lax.axis_index("state")
@@ -198,36 +198,27 @@
         lax.fori_loop(0, bands, first_band, 0)
 
     def two_squarings(pair, carry):
-        @pl.when(jnp.logical_and(late, pair > 0))
+        first = 2 * pair
+
+        @pl.when(jnp.logical_and(first > 0, first <= products))
         def _():
             multiply(whole, yh, yl, gh, gl, 0)
 
-        @pl.when(2 * pair < top)
-        def _():
-            square(mats, 2 * pair, 2 * pair + 1, gh, gl, 0)
-
-        @pl.when(late)
+        @pl.when(first < top)
+        def _():
+            square(mats, first, first + 1, gh, gl, 0)
+
+        @pl.when(first + 1 <= products)
         def _():
             multiply(whole, yh, yl, gh, gl, 1)
 
-        @pl.when(2 * pair + 1 < top)
-        def _():
-            square(mats, 2 * pair + 1, 2 * pair + 2, gh, gl, 1)
+        @pl.when(first + 1 < top)
+        def _():
+            square(mats, first + 1, first + 2, gh, gl, 1)
 
         return carry
 
     lax.fori_loop(0, lax.div(top + 1, 2), two_squarings, 0)
-
-    def one_product(q, carry):
-        def halve(i, inside):
-            gh[0, band(i), :], gl[0, band(i), :] = split(mats[q, band(i), :])
-            return inside
-
-        lax.fori_loop(0, bands, halve, 0)
-        multiply(whole, yh, yl, gh, gl, 0)
-        return carry
-
-    lax.fori_loop(1, jnp.where(late, 1, products + 1), one_product, 0)
 
     load_t.wait()
 
@@ -239,7 +230,8 @@
             device_id=(where, state), device_id_type=MESH_ID)
 
     mean_in = send(xout, xin, 0, following)
-    map_over = send(mats.at[M_SLOT], mats.at[OTHER_SLOT], 1, partner)
+    matrix_over = send(mats.at[M_SLOT], mats.at[OTHER_SLOT], 1, partner)
+    present_over = send(seen, other_seen, 3, partner)
     offset_over = send(offset, other_offset, 2, partner)
     hands = jnp.logical_and(ships, core == 0)
     takes = jnp.logical_and(ships, core == 1)
@@ -254,6 +246,14 @@
 
     def block(i):
         return pl.ds(pl.multiple_of(i * BLK, BLK), BLK)
+
+    offset[...] = observed
+    seen[...] = present
+
+    @pl.when(jnp.logical_and(hands, jnp.logical_not(has_map)))
+    def _():
+        offset_over.start()
+        present_over.start()
 
     @pl.when(has_gain)
     def _():
@@ -262,6 +262,11 @@
             left_high, left_low = split(mats[P_SLOT, rows, :] * present)
             for cols in column_parts(0, S):
                 mats[W_SLOT, rows, cols] = dot3(left_high, left_low, yh[:, cols], yl[:, cols])
+
+            @pl.when(jnp.logical_and(hands, jnp.logical_not(has_map)))
+            def _():
+                send(mats.at[W_SLOT, rows, :], mats.at[OTHER_SLOT, rows, :], 1, partner).start()
+
             gh[1, rows, :], gl[1, rows, :] = split(mats[W_SLOT, rows, :] * present)
             gh[0, rows, :], gl[0, rows, :] = split(mats[T_SLOT, rows, :])
             return carry
@@ -270,12 +275,6 @@
 
     @pl.when(has_map)
     def _():
-        offset[...] = matvec(mats, W_SLOT, observed)
-
-        @pl.when(hands)
-        def _():
-            offset_over.start()
-
         def map_rows(i, carry):
             rows = block(i)
             for cols in column_parts(0, S):
@@ -289,11 +288,20 @@
             return carry
 
         lax.fori_loop(0, S // BLK, map_rows, 0)
+        offset[...] = matvec(mats, W_SLOT, observed)
+
+        @pl.when(hands)
+        def _():
+            offset_over.start()
 
     @pl.when(takes)
     def _():
-        map_over.wait_recv()
+        matrix_over.wait_recv()
         offset_over.wait_recv()
+
+    @pl.when(jnp.logical_and(takes, jnp.logical_not(has_map)))
+    def _():
+        present_over.wait_recv()
 
     middle_out = send(xmid, xin, 0, partner)
     inner_out = send(xout, xin, 0, partner)
@@ -352,7 +360,7 @@
         lax.fori_loop(0, lax.div(series, 2), add_two, 0)
         xout[...] = moved + matvec(mats, P_SLOT, present * xcur[...])
 
-    @pl.when(jnp.logical_and(has_gain, jnp.logical_not(has_map)))
+    @pl.when(jnp.logical_and(has_gain, jnp.logical_not(jnp.logical_or(has_map, ships))))
     def _():
         moved = matvec(mats, T_SLOT, xin[...])
         xout[...] = moved + matvec(mats, W_SLOT, observed - present * moved)
@@ -361,7 +369,21 @@
     def _():
         xout[...] = matvec(mats, M_SLOT, xin[...]) + offset[...]
 
-    @pl.when(takes)
+    @pl.when(jnp.logical_and(takes, jnp.logical_not(has_map)))
+    def _():
+        moved = matvec(mats, T_SLOT, xin[...])
+        middle = moved + matvec(mats, OTHER_SLOT, other_offset[...] - other_seen[...] * moved)
+        xmid[...] = middle
+        moved = matvec(mats, T_SLOT, middle)
+        xout[...] = moved + matvec(mats, W_SLOT, observed - present * moved)
+
+        @pl.when(has_next)
+        def _():
+            mean_in.start()
+
+        middle_out.start()
+
+    @pl.when(jnp.logical_and(takes, has_map))
     def _():
         middle = matvec(mats, OTHER_SLOT, xin[...]) + other_offset[...]
         xmid[...] = middle
@@ -397,8 +419,12 @@
 
     @pl.when(hands)
     def _():
-        map_over.wait_send()
+        matrix_over.wait_send()
         offset_over.wait_send()
+
+    @pl.when(jnp.logical_and(hands, jnp.logical_not(has_map)))
+    def _():
+        present_over.wait_send()
 
     @pl.when(takes)
     def _():
@@ -419,8 +445,8 @@
         out_specs=vmem,
         scratch_shapes=[
             pltpu.VMEM((10, S, S), f32), pltpu.VMEM((1, S, S), f32), halves, halves, half, half,
-            *[vector] * 7, pltpu.VMEM((1, LANE), f32),
-            pltpu.SemaphoreType.DMA((S // LANE + 1,)), pltpu.SemaphoreType.DMA((3,)), pltpu.SemaphoreType.DMA((3,)),
+            *[vector] * 9, pltpu.VMEM((1, LANE), f32),
+            pltpu.SemaphoreType.DMA((S // LANE + 1,)), pltpu.SemaphoreType.DMA((4,)), pltpu.SemaphoreType.DMA((4,)),
             pltpu.SemaphoreType.REGULAR,
         ],
         compiler_params=pltpu.CompilerParams(

time: 109 us -> 105 us (0.963)
  Pallas kernels: 108 us -> 104 us
    pallas_call x1, Pallas kernels: 108 us -> 104 us  [per_device(): pl.pallas_call(functools.partial(kernel, planes), out_shape=jax.ShapeDtyp...]
where the time goes in v3:
time: 105 us
  Pallas kernels  104 us (99%)
  local copies, waits for them, and re-layouts  1.27 us (1%)
    pallas_call x1, Pallas kernels, per_device(): pl.pallas_call(functools.partial(kernel, planes), out_shape=jax.ShapeDtyp...  104 us

profile of v3, /device:TPU:481, one launch (start us, length us, event | category | flops | bytes accessed | tf_op | source)
XLA Modules:
  0.0 104.8 jit_solution(17261210487364309871)
XLA Ops:
  0.0 103.5 %shard_map.64 = f32[1,1024]{1,0:T(1,128)} custom-call(f32[1024,1024]{1,0:T(8,128)} %t_hbm.1, f32[1024,1024]{1,0:T(8,128)} %p_hbm.1, f32[1,1024]{1,0:T(1,128)} %bitcast.2, s32[1,1024]{1,0:T(1,128)} %mask_ref.1, f32[1,1024]{1,0:T(1,128)} %read_ref.1, f32[1,1024]{1,0:T(1,128)} %bitcast.3), custom_call_target="tpu_custom_call" | custom-call | tf_op jit(solution)/shard_map/pallas_call | solution.py:441
  103.6 1.3 %constant_dynamic-slice_fusion = f32[1,64]{1,0:T(1,128)} fusion(f32[1,1024]{1,0:T(1,128)} %shard_map.64, s32[]{:T(128)S(6)} %select_n.3), kind=kLoop, calls=%fused_computation | loop fusion | bytes 516 | tf_op jit(solution)/shard_map/dynamic_slice | solution.py:456

commit v4 on v3

--- a/solution.py
+++ b/solution.py
@@ -21,6 +21,7 @@
 GAIN_FROM = 7
 MAP_FROM = 10
 SHIP_FROM = 7
+JOIN_FROM = 12
 MESH_ID = pl.DeviceIdType.MESH
 
 
@@ -109,6 +110,7 @@
     has_gain = z >= GAIN_FROM
     has_map = z >= MAP_FROM
     ships = z >= SHIP_FROM
+    joins = jnp.logical_and(jnp.logical_and(core == 1, z >= JOIN_FROM), z < planes - 1)
     entry_core = ships.astype(jnp.int32)
     next_entry = (z + 1 >= SHIP_FROM).astype(jnp.int32)
     has_next = jnp.logical_and(core == 1, z < planes - 1)
@@ -303,6 +305,24 @@
     def _():
         present_over.wait_recv()
 
+    @pl.when(joins)
+    def _():
+        def halve_other(i, carry):
+            yh[band(i), :], yl[band(i), :] = split(mats[OTHER_SLOT, band(i), :])
+            return carry
+
+        lax.fori_loop(0, bands, halve_other, 0)
+
+        def join_rows(i, carry):
+            rows = block(i)
+            left_high, left_low = split(mats[M_SLOT, rows, :])
+            for cols in column_parts(0, S):
+                mats[W_SLOT, rows, cols] = dot3(left_high, left_low, yh[:, cols], yl[:, cols])
+            return carry
+
+        lax.fori_loop(0, S // BLK, join_rows, 0)
+        seen[...] = matvec(mats, M_SLOT, other_offset[...]) + offset[...]
+
     middle_out = send(xmid, xin, 0, partner)
     inner_out = send(xout, xin, 0, partner)
     inner = jnp.logical_and(jnp.logical_not(ships), core == 0)
@@ -383,16 +403,27 @@
 
         middle_out.start()
 
-    @pl.when(jnp.logical_and(takes, has_map))
+    @pl.when(jnp.logical_and(jnp.logical_and(takes, has_map), jnp.logical_not(joins)))
     def _():
         middle = matvec(mats, OTHER_SLOT, xin[...]) + other_offset[...]
         xmid[...] = middle
+
+        @pl.when(jnp.logical_not(has_next))
+        def _():
+            middle_out.start()
+
         xout[...] = matvec(mats, M_SLOT, middle) + offset[...]
 
         @pl.when(has_next)
         def _():
             mean_in.start()
-
+            middle_out.start()
+
+    @pl.when(joins)
+    def _():
+        xout[...] = matvec(mats, W_SLOT, xin[...]) + seen[...]
+        mean_in.start()
+        xmid[...] = matvec(mats, OTHER_SLOT, xin[...]) + other_offset[...]
         middle_out.start()
 
     @pl.when(inner)

time: 105 us -> 106 us (level)
  no operation moved by 1% of the time
where the time goes in v4:
time: 106 us; the launch traced here: 105 us
  Pallas kernels  104 us (98%)
  local copies, waits for them, and re-layouts  1.27 us (1%)
    pallas_call x1, Pallas kernels, per_device(): pl.pallas_call(functools.partial(kernel, planes), out_shape=jax.ShapeDtyp...  104 us

profile of v4, /device:TPU:481, one launch (start us, length us, event | category | flops | bytes accessed | tf_op | source)
XLA Modules:
  0.0 105.5 jit_solution(9133315176294257538)
XLA Ops:
  0.0 104.2 %shard_map.64 = f32[1,1024]{1,0:T(1,128)} custom-call(f32[1024,1024]{1,0:T(8,128)} %t_hbm.1, f32[1024,1024]{1,0:T(8,128)} %p_hbm.1, f32[1,1024]{1,0:T(1,128)} %bitcast.2, s32[1,1024]{1,0:T(1,128)} %mask_ref.1, f32[1,1024]{1,0:T(1,128)} %read_ref.1, f32[1,1024]{1,0:T(1,128)} %bitcast.3), custom_call_target="tpu_custom_call" | custom-call | tf_op jit(solution)/shard_map/pallas_call | solution.py:472
  104.2 1.3 %constant_dynamic-slice_fusion = f32[1,64]{1,0:T(1,128)} fusion(f32[1,1024]{1,0:T(1,128)} %shard_map.64, s32[]{:T(128)S(6)} %select_n.3), kind=kLoop, calls=%fused_computation | loop fusion | bytes 516 | tf_op jit(solution)/shard_map/dynamic_slice | solution.py:487
